TPU v7x, 512 devices: a whole 4x8x8 slice. The times are simulated.
512 devices in a mesh: dp: 16 (over y, z_hi), ctx: 32 (over z_lo, x, core).
Axes of the slice: x: 4, y: 8, z: 8 (z_hi: 2, z_lo: 4; z = z_hi * 4 + z_lo), core: 2. Of those that a mesh axis runs over, the one named last changes fastest.
Arguments:
- queries: bfloat16 [16, 8192, 512], P('dp', 'ctx'), may hold values from -6 to 6
- keys: bfloat16 [16, 8192, 512], P('dp', 'ctx'), may hold values from -6 to 6
- values: bfloat16 [16, 8192, 512], P('dp', 'ctx'), may hold values from -24 to 24
- out_grad: bfloat16 [16, 8192, 1024], P('dp', 'ctx'), may hold values from -6 to 6
- w_out: bfloat16 [512, 1024], replicated, may hold values from -0.25 to 0.25
- block_mask: int32 [16, 64, 3], P('dp'), may hold values 0 or 1
Outputs:
- output: bfloat16 [16, 8192, 1024], P('dp', 'ctx')
- query_grad: bfloat16 [16, 8192, 512], P('dp', 'ctx')
- key_grad: bfloat16 [16, 8192, 512], P('dp', 'ctx')
- value_grad: bfloat16 [16, 8192, 512], P('dp', 'ctx')
- weight_grad: float32 [512, 1024], P('ctx')
All inputs are finite; a program needn't handle non-finite values. No bound on the sum of `block_mask` on one device may be relied on, other than what follows from the above.
Results may differ from a plain program's by a relative error of at most 0.038.
Values may be sent and summed in bfloat16 or wider, within the bound.
A program may use at most 64 MiB of HBM per device.

v0:
```python
import jax
import jax.numpy as jnp
from jax import lax
from jax.sharding import PartitionSpec as P

HEADS = 8
HD = 64
BLK = 128
RAD = 1


big_negative = -1e30


def with_halo(block, sides, width):
    for axis, dim in sides:
        count = lax.axis_size(axis)
        forward = [(i, i + 1) for i in range(count - 1)]
        forward.append((count - 1, 0))
        backward = [(target, source) for source, target in forward]
        low = lax.ppermute(
            lax.slice_in_dim(block, block.shape[dim] - width, None, axis=dim), axis, forward
        )
        high = lax.ppermute(lax.slice_in_dim(block, 0, width, axis=dim), axis, backward)
        block = jnp.concatenate([low, block, high], axis=dim)
    return block


def shifted(value, axis, steps):
    count = lax.axis_size(axis)
    pairs = [(source, (source + steps) % count) for source in range(count)]
    return lax.ppermute(value, axis, pairs)


def allowed_keys(mask_rows):
    centre = (jnp.arange(2 * RAD + 1) == RAD)[None, :]
    allowed = (mask_rows == 1) | centre
    return jnp.repeat(allowed, BLK, axis=1)


def body(queries, keys, values, out_grad, w_out, block_mask):
    query_rows = queries[0]
    key_rows = keys[0]
    value_rows = values[0]
    grad_rows = out_grad[0]
    tok_count = query_rows.shape[0]
    feat_count = query_rows.shape[1]
    blocks_here = tok_count // BLK
    rim_rows = RAD * BLK
    span_rows = (2 * RAD + 1) * BLK
    group_width = 2 * HD
    score_scale = HD ** (-0.5)
    position = lax.axis_index("ctx")
    pattern = block_mask[0]
    pattern_pad = jnp.concatenate([pattern[-RAD:], pattern, pattern[:RAD]], axis=0)
    own_pattern = lax.dynamic_slice_in_dim(
        pattern_pad, position * blocks_here + RAD, blocks_here, 0
    )
    query_allow = allowed_keys(own_pattern)
    key_value = jnp.stack([key_rows, value_rows])
    extended = with_halo(key_value, (("ctx", 1),), rim_rows)
    windows = jnp.stack(
        [
            extended[:, row_block * BLK : row_block * BLK + span_rows]
            for row_block in range(blocks_here)
        ]
    )
    attn_grad = lax.dot_general(
        grad_rows, w_out, (((1,), (1,)), ((), ())), preferred_element_type=jnp.float32
    ).astype(jnp.bfloat16)
    attn_parts = []
    query_parts = []
    key_parts = []
    value_parts = []
    for head_group in range(HEADS // 2):
        columns = slice(head_group * group_width, (head_group + 1) * group_width)
        q_block = query_rows[:, columns].reshape(blocks_here, BLK, 2, HD)
        k_window = windows[:, 0, :, columns].reshape(blocks_here, span_rows, 2, HD)
        v_window = windows[:, 1, :, columns].reshape(blocks_here, span_rows, 2, HD)
        g_block = attn_grad[:, columns].reshape(blocks_here, BLK, 2, HD)
        scores = (
            jnp.einsum("bqhd,bkhd->bhqk", q_block, k_window, preferred_element_type=jnp.float32)
            * score_scale
        )
        scores = jnp.where(query_allow[:, None, None, :], scores, big_negative)
        row_max = jnp.max(scores, axis=-1, keepdims=True)
        log_total = row_max + jnp.log(jnp.sum(jnp.exp(scores - row_max), axis=-1, keepdims=True))
        probs = jnp.exp(scores - log_total)
        probs_bf = probs.astype(jnp.bfloat16)
        attn_block = jnp.einsum(
            "bhqk,bkhd->bqhd", probs_bf, v_window, preferred_element_type=jnp.float32
        ).astype(jnp.bfloat16)
        row_delta = jnp.sum(g_block.astype(jnp.float32) * attn_block.astype(jnp.float32), axis=-1)
        row_delta = jnp.transpose(row_delta, (0, 2, 1))[..., None]
        dprob = jnp.einsum("bqhd,bkhd->bhqk", g_block, v_window, preferred_element_type=jnp.float32)
        dscore = (probs * (dprob - row_delta) * score_scale).astype(jnp.bfloat16)
        query_part = jnp.einsum(
            "bhqk,bkhd->bqhd", dscore, k_window, preferred_element_type=jnp.float32
        )
        attn_parts.append(attn_block.reshape(tok_count, group_width))
        query_parts.append(query_part.reshape(tok_count, group_width).astype(jnp.bfloat16))
        key_window_part = jnp.einsum(
            "bhqk,bqhd->bkhd", dscore, q_block, preferred_element_type=jnp.float32
        )
        value_window_part = jnp.einsum(
            "bhqk,bqhd->bkhd", probs_bf, g_block, preferred_element_type=jnp.float32
        )
        key_parts.append(key_window_part.reshape(blocks_here, span_rows, group_width))
        value_parts.append(value_window_part.reshape(blocks_here, span_rows, group_width))
    attn = jnp.concatenate(attn_parts, axis=1)
    output = jnp.dot(attn, w_out, preferred_element_type=jnp.float32).astype(jnp.bfloat16)
    query_grad = jnp.concatenate(query_parts, axis=1)
    key_windows = jnp.concatenate(key_parts, axis=2)
    value_windows = jnp.concatenate(value_parts, axis=2)
    window_pairs = jnp.stack([key_windows, value_windows], axis=1)
    window_sums = jnp.zeros((2, tok_count + 2 * rim_rows, feat_count), jnp.float32)
    for row_block in range(blocks_here):
        first_row = row_block * BLK
        window_sums = window_sums.at[:, first_row : first_row + span_rows].add(
            window_pairs[row_block]
        )
    from_right = shifted(window_sums[:, :rim_rows], "ctx", -1)
    from_left = shifted(window_sums[:, rim_rows + tok_count :], "ctx", 1)
    own_sums = window_sums[:, rim_rows : rim_rows + tok_count]
    own_sums = own_sums.at[:, tok_count - rim_rows :].add(from_right)
    own_sums = own_sums.at[:, :rim_rows].add(from_left)
    key_grad = own_sums[0].astype(jnp.bfloat16)
    value_grad = own_sums[1].astype(jnp.bfloat16)
    weight_share = lax.psum_scatter(
        lax.dot_general(
            attn, grad_rows, (((0,), (0,)), ((), ())), preferred_element_type=jnp.float32
        ),
        "ctx",
        scatter_dimension=0,
        tiled=True,
    )
    weight_total = lax.psum(weight_share, "dp")
    weight_grad = weight_total * (lax.axis_size("dp") * tok_count * lax.axis_size("ctx")) ** (-0.5)
    return (output[None], query_grad[None], key_grad[None], value_grad[None], weight_grad)


def solution(mesh):
    placed = (
        P("dp", "ctx", None),
        P("dp", "ctx", None),
        P("dp", "ctx", None),
        P("dp", "ctx", None),
        P(),
        P("dp", None, None),
    )
    return jax.shard_map(
        body,
        mesh=mesh,
        in_specs=placed,
        out_specs=(
            P("dp", "ctx", None),
            P("dp", "ctx", None),
            P("dp", "ctx", None),
            P("dp", "ctx", None),
            P("ctx", None),
        ),
        check_vma=False,
    )
```

profile of v0, /device:TPU:2, one launch (start us, length us, event | category | flops | bytes accessed | tf_op | source)
XLA Modules:
  0.0 401.2 jit_solution(2695759000667080218)
XLA Ops:
  7.2 1.1 constant_dynamic-update-slice_fusion.1
  8.3 1.0 constant_dynamic-update-slice_fusion
  9.3 0.7 fusion.64
  10.0 1.9 collective-permute-start.1
  12.0 2.4 collective-permute-start
  14.8 0.5 convolution_convert_fusion.1
  16.5 0.7 copy.74
  17.5 0.7 copy.62
  18.3 0.7 copy.56
  19.0 4.9 %collective-permute-done = bf16[2,128,512]{2,1,0:T(8,128)(2,1)S(1)} collective-permute-done((bf16[2,128,512]{2,1,0:T(8,128)(2,1)S(1)}, bf16[2,128,512]{2,1,0:T(8,128)(2,1)S(1)}, u32[]{:S(2)}, u32[]{:S(2)}) %collective-permute-start) | collective-permute-done | bytes 262176 | tf_op jit(solution)/shard_map/ppermute | solution.py:21
  24.1 0.4 pad_maximum_fusion.1
  24.6 0.2 copy.66
  24.8 0.4 fusion.70
  25.3 0.3 fusion.52
  25.6 0.9 multiply_reduce_fusion.1
  26.5 0.3 fusion.22
  26.9 0.9 fusion.31
  27.7 0.3 fusion.74
  28.0 0.8 copy.72
  29.6 0.8 copy.71
  30.4 1.5 copy.70
  32.0 0.9 copy.111
  32.9 0.9 copy.94
  33.8 0.6 copy.187
  34.4 0.9 copy.123
  35.3 0.3 fusion.69
  35.8 0.3 multiply_reduce_fusion.2
  36.2 1.1 fusion.21
  37.3 0.4 fusion.68
  37.8 0.3 multiply_reduce_fusion.3
  38.3 0.4 fusion.71
  38.8 0.9 multiply_reduce_fusion
  39.8 0.7 copy-done.17
  40.5 1.8 fusion.39
  42.4 2.0 fusion.73
  44.4 1.9 copy.110
  46.3 1.9 fusion.55
  48.2 1.9 copy.122
  50.1 1.3 fusion.20
  51.4 1.0 fusion.72
  52.5 1.9 copy.109
  54.4 1.1 fusion.58
  55.5 1.9 copy.121
  57.4 0.3 fusion.23
  57.8 1.1 fusion.75
  58.8 2.0 copy.112
  60.8 1.1 fusion.49
  61.8 1.1 copy.124
  63.0 1.4 maximum_bitcast_fusion
  64.9 2.7 collective-permute-start.2
  67.7 0.2 fusion.30
  68.0 0.2 fusion.29
  68.3 0.3 fusion
  68.7 6.1 %collective-permute-done.2 = f32[2,128,512]{2,1,0:T(8,128)S(1)} collective-permute-done((f32[2,128,512]{2,1,0:T(8,128)S(1)}, f32[2,128,512]{2,1,0:T(8,128)S(1)}, u32[]{:S(2)}, u32[]{:S(2)}) %collective-permute-start.2) | collective-permute-done | bytes 524320 | tf_op jit(solution)/shard_map/ppermute | solution.py:32
  75.0 2.1 collective-permute-start.3
  77.0 0.2 fusion.32
  77.4 0.8 copy.125
  78.2 1.3 fusion.24
  79.5 7.5 %collective-permute-done.3 = f32[2,128,512]{2,1,0:T(8,128)} collective-permute-done((f32[2,128,512]{2,1,0:T(8,128)S(1)}, f32[2,128,512]{2,1,0:T(8,128)}, u32[]{:S(2)}, u32[]{:S(2)}) %collective-permute-start.3) | collective-permute-done | bytes 524320 | tf_op jit(solution)/shard_map/ppermute | solution.py:32
  87.0 1.2 fusion.37
  88.2 105.4 %reduce-scatter.2.cloned.1.call-done = f32[16,1024]{1,0:T(8,128)} async-done(((f32[512,1024]{1,0:T(8,128)}), f32[16,1024]{1,0:T(8,128)}) %reduce-scatter.2.cloned.1.call-update) | async-done | bytes 65552 | tf_op jit(solution)/shard_map/reduce_scatter | solution.py:129
  193.7 0.8 fusion.63
  194.5 198.4 %all-reduce.3.cloned.1.call-done = f32[16,1024]{1,0:T(8,128)} async-done(((f32[16,1024]{1,0:T(8,128)}), f32[16,1024]{1,0:T(8,128)}) %all-reduce.3.cloned.1.call-update) | async-done | bytes 65552 | tf_op jit(solution)/shard_map/psum | solution.py:137
  392.9 1.5 broadcast_multiply_fusion
  (122 shorter events, 4.9 us)
Async XLA Ops:
  7.2 7.6 %copy-start = (bf16[512,1024]{1,0:T(8,128)(2,1)S(1)}, bf16[512,1024]{1,0:T(8,128)(2,1)}, u32[]{:S(2)}) copy-start(bf16[512,1024]{1,0:T(8,128)(2,1)} %param.18) | copy-start | bytes 3145732
  7.2 7.2 %copy-start.28 = (s32[1,64,3]{1,0,2:T(1,128)S(1)}, s32[1,64,3]{1,0,2:T(1,128)}, u32[]{:S(2)}) copy-start(s32[1,64,3]{1,0,2:T(1,128)} %param.19) | copy-start | bytes 2308
  7.2 7.6 %copy-start.2 = (bf16[1,256,1024]{2,1,0:T(8,128)(2,1)S(1)}, bf16[1,256,1024]{2,1,0:T(8,128)(2,1)}, u32[]{:S(2)}) copy-start(bf16[1,256,1024]{2,1,0:T(8,128)(2,1)} %param.17) | copy-start | bytes 1572868
  7.2 186.4 %reduce-scatter.2.cloned.1.call-start = ((), (), s32[]{:S(2)}) async-start(), calls=%async_computation.1 | async-start | bytes 2162688 | tf_op jit(solution)/shard_map/reduce_scatter | solution.py:129
  10.0 9.0 %collective-permute-start.1 = (bf16[2,128,512]{2,1,0:T(8,128)(2,1)}, bf16[2,128,512]{2,1,0:T(8,128)(2,1)S(1)}, u32[]{:S(2)}, u32[]{:S(2)}) collective-permute-start(bf16[2,128,512]{2,1,0:T(8,128)(2,1)} %get-tuple-element.72), channel_id=1, source_target_pairs={{1,0},{2,1},{3,2},{4,3},{5,4},{6,5},{7,6},{8,7},{9,8},{10,9},{11,1... | collective-permute-start | bytes 786440 | tf_op jit(solution)/shard_map/ppermute | solution.py:24
  12.0 12.0 %collective-permute-start = (bf16[2,128,512]{2,1,0:T(8,128)(2,1)S(1)}, bf16[2,128,512]{2,1,0:T(8,128)(2,1)S(1)}, u32[]{:S(2)}, u32[]{:S(2)}) collective-permute-start(bf16[2,128,512]{2,1,0:T(8,128)(2,1)S(1)} %get-tuple-element.73), channel_id=1, source_target_pairs={{0,1},{1,2},{2,3},{3,4},{4,5},{5,6},{6,7},{7,8},{8,9},{9,10},{10,1... | collective-permute-start | bytes 786440 | tf_op jit(solution)/shard_map/ppermute | solution.py:21
  14.8 1.5 copy-start.25
  16.3 19.9 %copy-start.19 = (bf16[2,128,2,64]{1,3,2,0:T(8,128)(2,1)}, bf16[2,128,2,64]{1,3,2,0:T(8,128)(2,1)S(1)}, u32[]{:S(2)}) copy-start(bf16[2,128,2,64]{1,3,2,0:T(8,128)(2,1)S(1)} %copy.84) | copy-start | bytes 196612
  29.0 8.8 %copy-start.12 = (bf16[2,1,384,128]{2,3,0,1:T(8,128)(2,1)}, bf16[2,1,384,128]{2,3,0,1:T(8,128)(2,1)S(1)}, u32[]{:S(2)}) copy-start(bf16[2,1,384,128]{2,3,0,1:T(8,128)(2,1)S(1)} %copy.50) | copy-start | bytes 589828
  29.2 8.1 %copy-start.6 = (bf16[2,1,384,128]{2,3,0,1:T(8,128)(2,1)}, bf16[2,1,384,128]{2,3,0,1:T(8,128)(2,1)S(1)}, u32[]{:S(2)}) copy-start(bf16[2,1,384,128]{2,3,0,1:T(8,128)(2,1)S(1)} %copy.54) | copy-start | bytes 589828
  29.2 6.1 %copy-start.24 = (bf16[2,128,2,64]{1,3,2,0:T(8,128)(2,1)S(1)}, bf16[2,128,2,64]{1,3,2,0:T(8,128)(2,1)}, u32[]{:S(2)}) copy-start(bf16[2,128,2,64]{1,3,2,0:T(8,128)(2,1)} %copy.62) | copy-start | bytes 196612
  29.6 6.1 %copy-start.8 = (bf16[2,1,384,128]{2,3,0,1:T(8,128)(2,1)}, bf16[2,1,384,128]{2,3,0,1:T(8,128)(2,1)S(1)}, u32[]{:S(2)}) copy-start(bf16[2,1,384,128]{2,3,0,1:T(8,128)(2,1)S(1)} %copy.60) | copy-start | bytes 589828
  35.7 1.6 copy-start.22
  37.3 0.9 copy-start.4
  37.3 0.9 copy-start.20
  37.8 1.0 copy-start.10
  38.2 1.5 copy-start.26
  38.3 2.3 copy-start.3
  39.8 0.7 copy-start.17
  42.3 350.6 %all-reduce.3.cloned.1.call-start = ((), (), s32[]{:S(2)}) async-start(), calls=%async_computation.2 | async-start | bytes 131072 | tf_op jit(solution)/shard_map/psum | solution.py:137
  48.2 3.2 copy-start.23
  52.5 4.9 %copy-start.11 = (bf16[2,1,384,128]{2,3,0,1:T(8,128)(2,1)S(1)}, bf16[2,1,384,128]{2,3,0,1:T(8,128)(2,1)}, u32[]{:S(2)}) copy-start(bf16[2,1,384,128]{2,3,0,1:T(8,128)(2,1)} %copy.71) | copy-start | bytes 589828
  52.5 4.9 %copy-start.29 = (f32[2,128,2]{1,2,0:T(2,128)S(1)}, f32[2,128,2]{1,2,0:T(2,128)}, u32[]{:S(2)}) copy-start(f32[2,128,2]{1,2,0:T(2,128)} %get-tuple-element.92) | copy-start | bytes 6148
  54.4 3.3 copy-start.21
  58.8 4.2 %copy-start.13 = (f32[2,384,128]{2,1,0:T(8,128)S(1)}, f32[2,384,128]{2,1,0:T(8,128)}, u32[]{:S(2)}) copy-start(f32[2,384,128]{2,1,0:T(8,128)} %copy.111) | copy-start | bytes 1179652
  63.0 1.5 copy-start.14
  63.0 1.5 copy-start.15
  63.0 1.6 copy-start.16
  64.7 2.9 copy-start.1
  64.7 2.9 copy-start.9
  64.9 3.1 copy-start.7
  64.9 9.9 %collective-permute-start.2 = (f32[2,128,512]{2,1,0:T(8,128)S(1)}, f32[2,128,512]{2,1,0:T(8,128)S(1)}, u32[]{:S(2)}, u32[]{:S(2)}) collective-permute-start(f32[2,128,512]{2,1,0:T(8,128)S(1)} %slice.252), channel_id=1, source_target_pairs={{0,31},{1,0},{2,1},{3,2},{4,3},{5,4},{6,5},{7,6},{8,7},{9,8},{10,9... | collective-permute-start | bytes 1572872 | tf_op jit(solution)/shard_map/ppermute | solution.py:32
  68.7 8.4 %copy-start.5 = (bf16[2,1,384,128]{2,3,0,1:T(8,128)(2,1)S(1)}, bf16[2,1,384,128]{2,3,0,1:T(8,128)(2,1)}, u32[]{:S(2)}) copy-start(bf16[2,1,384,128]{2,3,0,1:T(8,128)(2,1)} %copy.72) | copy-start | bytes 589828
  68.7 8.7 %copy-start.27 = (bf16[16,8,2,128]{3,1,2,0:T(8,128)(2,1)S(1)}, bf16[16,8,2,128]{3,1,2,0:T(8,128)(2,1)}, u32[]{:S(2)}) copy-start(bf16[16,8,2,128]{3,1,2,0:T(8,128)(2,1)} %copy.187) | copy-start | bytes 196612
  74.9 3.3 copy-start.18
  75.0 12.0 %collective-permute-start.3 = (f32[2,128,512]{2,1,0:T(8,128)S(1)}, f32[2,128,512]{2,1,0:T(8,128)}, u32[]{:S(2)}, u32[]{:S(2)}) collective-permute-start(f32[2,128,512]{2,1,0:T(8,128)S(1)} %get-tuple-element.58), channel_id=1, source_target_pairs={{0,1},{1,2},{2,3},{3,4},{4,5},{5,6},{6,7},{7,8},{8,9},{9,10},{10,1... | collective-permute-start | bytes 1572872 | tf_op jit(solution)/shard_map/ppermute | solution.py:32
Sparse Core Ops, SparseCore 0:
  42.4 151.1 reduce-scatter.1
  196.8 195.9 all-reduce.2
where the time goes:
time: 402 us; the launch traced here: 401 us
  waiting for transfers between devices  322 us (80%)
  local copies, waits for them, and re-layouts  28.3 us (7%)
  matrix products  20.6 us (5%)
  between operations  14.8 us (4%)
  starting transfers between devices  9.14 us (2%)
  other arithmetic  6.03 us (2%)
    psum x1, waiting for transfers between devices, body(): weight_total = lax.psum(weight_share, 'dp')  198 us
    reduce_scatter x1, waiting for transfers between devices, body(): lax.psum_scatter(lax.dot_general(attn, grad_rows, (((0,), (0,)), ((), ())...  105 us
    ppermute x2, waiting for transfers between devices, shifted(): return lax.ppermute(value, axis, pairs)  13.6 us
  transfers between devices with their start and end apart: 6, of which 5 were waited for; matrix products, arithmetic and copies ran while one was open for 8% of the time, Pallas kernels for 0%

commit v1 on v0

v1 whole, which is shorter than its diff:
```python
import functools

import jax
import jax.numpy as jnp
from jax import lax
from jax.experimental import pallas as pl
from jax.experimental.pallas import tpu as pltpu
from jax.sharding import PartitionSpec as P

HD = 64
BLK = 128
GW = 2 * HD
NG = 4
WIN = 3 * BLK
BF = jnp.bfloat16
F32 = jnp.float32
MESH = pl.DeviceIdType.MESH
NEG = -1e30


def nn(a, b):
    return lax.dot_general(a, b, (((1,), (0,)), ((), ())), preferred_element_type=F32)


def nt(a, b):
    return lax.dot_general(a, b, (((1,), (1,)), ((), ())), preferred_element_type=F32)


def block_diag(rows):
    lane = lax.broadcasted_iota(jnp.int32, rows.shape, 1)
    zero = jnp.zeros_like(rows)
    return jnp.concatenate([jnp.where(lane < HD, rows, zero), jnp.where(lane < HD, zero, rows)], axis=0)


def diagonal(both):
    return jnp.concatenate([both[:HD, :BLK], both[HD:, BLK:]], axis=0)


def kernel(
    dims, wscale,
    q_hbm, k_hbm, v_hbm, g_hbm, w_hbm, mask,
    out_s, dq_s, dk_s, dv_s, dw_out,
    q_s, k_ext, v_ext, g_s, w_s, k_t, v_t, da_t, qbd, abd, p_t, at, dw_own,
    csend, crecv, xsend, xrecv, ysend, yrecv, zsend, zrecv,
    dk_acc, dv_acc, gsend, grecv, dq_t,
    lsem, h_s, h_r, c_s, c_r, x_s, x_r, y_s, y_r, z_s, z_r, a_s, a_r, g_ss, g_rs,
):
    NY, ZH, ZL, NX = dims
    NZ = ZL * ZH
    CTX = ZL * NX * 2
    dp = lax.axis_index("dp")
    ctx = lax.axis_index("ctx")
    y, zh = dp // ZH, dp % ZH
    zl, x, core = ctx // (NX * 2), (ctx // 2) % NX, ctx % 2
    z = zh * ZL + zl

    def ident(y_, z_, x_, c_):
        return (y_ * ZH + z_ // ZL, (z_ % ZL) * (NX * 2) + x_ * 2 + c_)

    right = (dp, (ctx + 1) % CTX)
    left = (dp, (ctx + CTX - 1) % CTX)
    mate = (dp, ctx + 1 - 2 * core)
    x_peer = [ident(y, z, (x + d) % NX, core) for d in range(1, NX)]
    y_peer = [ident((y + d) % NY, z, x, core) for d in range(1, NY)]
    z_peer = [ident(y, (z + d) % NZ, x, core) for d in range(1, NZ)]

    def remote(src, dst, ssem, rsem, dev):
        return pltpu.make_async_remote_copy(
            src_ref=src, dst_ref=dst, send_sem=ssem, recv_sem=rsem, device_id=dev, device_id_type=MESH
        )

    barrier = pltpu.get_barrier_semaphore()
    peers = [right, left] + x_peer + y_peer + z_peer
    for dev in peers:
        pl.semaphore_signal(barrier, inc=1, device_id=dev, device_id_type=MESH)

    own = pl.ds(BLK, 2 * BLK)
    load_g = pltpu.make_async_copy(g_hbm, g_s, lsem.at[0])
    load_w = pltpu.make_async_copy(w_hbm, w_s, lsem.at[1])
    load_q = pltpu.make_async_copy(q_hbm, q_s, lsem.at[2])
    load_k = pltpu.make_async_copy(k_hbm, k_ext.at[own], lsem.at[3])
    load_v = pltpu.make_async_copy(v_hbm, v_ext.at[own], lsem.at[4])
    loads = [load_g, load_w, load_q, load_k, load_v]
    for copy in loads:
        copy.start()

    pl.semaphore_wait(barrier, len(peers))

    first, last = pl.ds(0, BLK), pl.ds(BLK, BLK)
    low, high = pl.ds(0, BLK), pl.ds(3 * BLK, BLK)
    halo = [
        remote(k_hbm.at[last], k_ext.at[low], h_s.at[0], h_r.at[0], right),
        remote(k_hbm.at[first], k_ext.at[high], h_s.at[1], h_r.at[1], left),
        remote(v_hbm.at[last], v_ext.at[low], h_s.at[2], h_r.at[2], right),
        remote(v_hbm.at[first], v_ext.at[high], h_s.at[3], h_r.at[3], left),
    ]
    for copy in halo:
        copy.start()

    def cols(g):
        return slice(g * GW, (g + 1) * GW)

    load_g.wait()
    load_w.wait()
    da = nt(g_s[...], w_s[...]).astype(BF)
    for b in range(2):
        for g in range(NG):
            abd[b, g] = block_diag(da[b * BLK:(b + 1) * BLK, cols(g)])
    da_t[...] = nt(w_s[...], g_s[...]).astype(BF)
    load_q.wait()
    for b in range(2):
        for g in range(NG):
            scaled = q_s[b * BLK:(b + 1) * BLK, cols(g)] * jnp.asarray(HD ** -0.5, BF)
            qbd[b, g] = block_diag(scaled)
    load_k.wait()
    load_v.wait()
    k_t[:, BLK:3 * BLK] = k_ext[BLK:3 * BLK, :].T
    v_t[:, BLK:3 * BLK] = v_ext[BLK:3 * BLK, :].T

    bias = []
    for b in range(2):
        row = ctx * 2 + b
        bias.append([jnp.where(mask[c, row] == 1, 0.0, NEG).astype(F32) for c in (0, 2)])

    for copy in halo:
        copy.wait_recv()
    k_t[:, :BLK] = k_ext[:BLK, :].T
    k_t[:, 3 * BLK:] = k_ext[3 * BLK:, :].T
    v_t[:, :BLK] = v_ext[:BLK, :].T
    v_t[:, 3 * BLK:] = v_ext[3 * BLK:, :].T

    def window(b):
        return slice(b * BLK, b * BLK + WIN)

    def forward(g):
        parts = []
        for b in range(2):
            s = nt(k_ext[window(b), cols(g)], qbd[b, g])
            lo, mid, hi = s[:BLK], s[BLK:2 * BLK], s[2 * BLK:]
            b_lo, b_hi = bias[b]
            top = jnp.maximum(
                jnp.max(mid, axis=0, keepdims=True),
                jnp.maximum(jnp.max(lo, axis=0, keepdims=True) + b_lo, jnp.max(hi, axis=0, keepdims=True) + b_hi),
            )
            e_lo = jnp.exp(lo - (top - b_lo))
            e_mid = jnp.exp(mid - top)
            e_hi = jnp.exp(hi - (top - b_hi))
            total = jnp.sum(e_lo + e_mid + e_hi, axis=0, keepdims=True)
            inv = 1.0 / total
            p = jnp.concatenate([(e_lo * inv).astype(BF), (e_mid * inv).astype(BF), (e_hi * inv).astype(BF)], axis=0)
            p_t[b, g] = p
            parts.append(diagonal(nn(v_t[cols(g), window(b)], p)).astype(BF))
        rows = jnp.concatenate(parts, axis=1)
        at[g] = rows.reshape(4, 2, 16, 2 * BLK)

    def core_copy(g):
        return remote(csend.at[g], crecv.at[g], c_s.at[g], c_r.at[g], mate)

    def x_copy(g, d):
        return remote(xsend.at[g, (x + d) % NX], xrecv.at[g, d - 1], x_s.at[g, d - 1], x_r.at[g, d - 1], x_peer[d - 1])

    def y_copy(g, d):
        return remote(ysend.at[g, (y + d) % NY], yrecv.at[g, d - 1], y_s.at[g, d - 1], y_r.at[g, d - 1], y_peer[d - 1])

    def z_copy(d):
        return remote(zsend.at[(z + d) % ZL], zrecv.at[d - 1], z_s.at[d - 1], z_r.at[d - 1], z_peer[d - 1])

    own_cols = pl.ds(pl.multiple_of(y * BLK, BLK), BLK)

    def a_copy(d):
        return remote(dw_out.at[:, own_cols], dw_out.at[:, own_cols], a_s.at[d - 1], a_r.at[d - 1], y_peer[d - 1])

    def a_arrival(d):
        there = pl.ds(pl.multiple_of(((y + NY - d) % NY) * BLK, BLK), BLK)
        return remote(dw_out.at[:, own_cols], dw_out.at[:, there], a_s.at[d - 1], a_r.at[d - 1], y_peer[d - 1])

    def weight_part(g):
        mine = at[g, :, core].reshape(64, 2 * BLK)
        other = at[g, :, 1 - core].reshape(64, 2 * BLK)
        part = nn(jnp.concatenate([mine, other], axis=0), g_s[...])
        csend[g] = part[64:].astype(BF)
        dw_own[g] = part[:64]
        core_copy(g).start()

    def core_sum(g):
        core_copy(g).wait_recv()
        total = dw_own[g] + crecv[g].astype(F32)
        xsend[g] = total.astype(BF).reshape(4, 16, 1024)
        for d in range(1, NX):
            x_copy(g, d).start()

    def x_sum(g):
        total = xsend[g, x].astype(F32)
        for d in range(1, NX):
            x_copy(g, d).wait_recv()
            total += xrecv[g, d - 1].astype(F32)
        total = total.astype(BF)
        for j in range(8):
            ysend[g, j] = total[:, j * BLK:(j + 1) * BLK]
        for d in range(1, NY):
            y_copy(g, d).start()

    def y_sum(g):
        total = ysend[g, y].astype(F32)
        for d in range(1, NY):
            y_copy(g, d).wait_recv()
            total += yrecv[g, d - 1].astype(F32)
        zsend[g] = total

    def z_start():
        for d in range(1, NZ):
            z_copy(d).start()

    def z_sum():
        total = zsend[z % ZL]
        for d in range(1, NZ):
            z_copy(d).wait_recv()
            total += zrecv[d - 1]
        dw_out[:, own_cols] = total * wscale
        for d in range(1, NY):
            a_copy(d).start()

    def grad_copy(side, g):
        return remote(gsend.at[side, g], grecv.at[side, g], g_ss.at[side, g], g_rs.at[side, g], right if side else left)

    def backward(g):
        tok = [slice(0, BLK), slice(BLK, 2 * BLK)]
        k_win, v_win = [], []
        rows = at[g].reshape(GW, 2 * BLK)
        q_parts = []
        for b in range(2):
            prod = rows[:, tok[b]].astype(F32) * da_t[cols(g), tok[b]].astype(F32)
            delta = jnp.concatenate(
                [jnp.sum(prod[:HD], axis=0, keepdims=True), jnp.sum(prod[HD:], axis=0, keepdims=True)], axis=1
            )
            dp_t = nt(v_ext[window(b), cols(g)], abd[b, g])
            p = p_t[b, g]
            ds = (p.astype(F32) * (dp_t - delta)).astype(BF)
            v_win.append(nn(p, abd[b, g]))
            k_win.append(nn(ds, qbd[b, g]))
            q_parts.append((diagonal(nn(k_t[cols(g), window(b)], ds)) * (HD ** -0.5)).astype(BF))
        for n, win in enumerate((k_win, v_win)):
            gsend[0, g, n] = win[0][:BLK].astype(BF)
            gsend[1, g, n] = win[1][2 * BLK:].astype(BF)
        grad_copy(0, g).start()
        grad_copy(1, g).start()
        dk_acc[g] = k_win[0][BLK:] + k_win[1][:2 * BLK]
        dv_acc[g] = v_win[0][BLK:] + v_win[1][:2 * BLK]
        dq_t[cols(g), :] = jnp.concatenate(q_parts, axis=1)

    for g in range(NG):
        forward(g)
        weight_part(g)
        if g >= 1:
            core_sum(g - 1)
    for g in range(NG):
        backward(g)
        if g == 0:
            core_sum(NG - 1)
        x_sum(g)
        if g >= 1:
            y_sum(g - 1)

    dq_s[...] = dq_t[...].T
    y_sum(NG - 1)
    z_start()
    attn = at[...].reshape(NG * GW, 2 * BLK).T
    out_s[...] = nn(attn, w_s[...]).astype(BF)
    z_sum()
    for g in range(NG):
        grad_copy(0, g).wait_recv()
        grad_copy(1, g).wait_recv()
        for n, (acc, dst) in enumerate(((dk_acc, dk_s), (dv_acc, dv_s))):
            dst[:BLK, cols(g)] = (acc[g, :BLK] + grecv[1, g, n].astype(F32)).astype(BF)
            dst[BLK:, cols(g)] = (acc[g, BLK:] + grecv[0, g, n].astype(F32)).astype(BF)
    for d in range(1, NY):
        a_arrival(d).wait_recv()

    for copy in halo:
        copy.wait_send()
    for g in range(NG):
        core_copy(g).wait_send()
        for d in range(1, NX):
            x_copy(g, d).wait_send()
        for d in range(1, NY):
            y_copy(g, d).wait_send()
        grad_copy(0, g).wait_send()
        grad_copy(1, g).wait_send()
    for d in range(1, NZ):
        z_copy(d).wait_send()
    for d in range(1, NY):
        a_copy(d).wait_send()


def body(dims, wscale, queries, keys, values, out_grad, w_out, block_mask):
    NY, ZH, ZL, NX = dims
    NZ = ZL * ZH
    tok, feat = queries.shape[1:]
    width = w_out.shape[1]
    hbm = pl.BlockSpec(memory_space=pl.ANY)
    vm = pltpu.VMEM
    dma = pltpu.SemaphoreType.DMA
    nx, ny, nz = max(NX - 1, 1), max(NY - 1, 1), max(NZ - 1, 1)
    outs = pl.pallas_call(
        functools.partial(kernel, dims, wscale),
        out_shape=(
            jax.ShapeDtypeStruct((tok, width), BF),
            jax.ShapeDtypeStruct((tok, feat), BF),
            jax.ShapeDtypeStruct((tok, feat), BF),
            jax.ShapeDtypeStruct((tok, feat), BF),
            jax.ShapeDtypeStruct((16, width), F32),
        ),
        in_specs=[hbm] * 5 + [pl.BlockSpec(memory_space=pltpu.SMEM)],
        out_specs=[pl.BlockSpec(memory_space=pltpu.VMEM)] * 5,
        scratch_shapes=[
            vm((tok, feat), BF),
            vm((4 * BLK, feat), BF),
            vm((4 * BLK, feat), BF),
            vm((tok, width), BF),
            vm((feat, width), BF),
            vm((feat, 4 * BLK), BF),
            vm((feat, 4 * BLK), BF),
            vm((feat, tok), BF),
            vm((2, NG, 2 * BLK, GW), BF),
            vm((2, NG, 2 * BLK, GW), BF),
            vm((2, NG, WIN, 2 * BLK), BF),
            vm((NG, 4, 2, 16, tok), BF),
            vm((NG, 64, width), F32),
            vm((NG, 64, width), BF),
            vm((NG, 64, width), BF),
            vm((NG, 4, 16, width), BF),
            vm((NG, nx, 16, width), BF),
            vm((NG, 8, 16, BLK), BF),
            vm((NG, ny, 16, BLK), BF),
            vm((NG, 16, BLK), F32),
            vm((nz, 16, BLK), F32),
            vm((NG, tok, GW), F32),
            vm((NG, tok, GW), F32),
            vm((2, NG, 2, BLK, GW), BF),
            vm((2, NG, 2, BLK, GW), BF),
            vm((feat, tok), BF),
            dma((5,)),
            dma((4,)), dma((4,)),
            dma((NG,)), dma((NG,)),
            dma((NG, nx)), dma((NG, nx)),
            dma((NG, ny)), dma((NG, ny)),
            dma((nz,)), dma((nz,)),
            dma((ny,)), dma((ny,)),
            dma((2, NG)), dma((2, NG)),
        ],
        compiler_params=pltpu.CompilerParams(
            collective_id=0, has_side_effects=True, vmem_limit_bytes=60 * 1024 * 1024
        ),
    )(queries[0], keys[0], values[0], out_grad[0], w_out, block_mask[0].T)
    return (outs[0][None], outs[1][None], outs[2][None], outs[3][None], outs[4])


def solution(mesh, dims=(8, 2, 4, 4)):
    tokens = mesh.shape["dp"] * mesh.shape["ctx"] * 256
    placed = (
        P("dp", "ctx", None),
        P("dp", "ctx", None),
        P("dp", "ctx", None),
        P("dp", "ctx", None),
        P(),
        P("dp", None, None),
    )
    return jax.shard_map(
        functools.partial(body, dims, tokens ** -0.5),
        mesh=mesh,
        in_specs=placed,
        out_specs=(
            P("dp", "ctx", None),
            P("dp", "ctx", None),
            P("dp", "ctx", None),
            P("dp", "ctx", None),
            P("ctx", None),
        ),
        check_vma=False,
    )
```

time: 402 us -> 60.3 us (0.15)
  the two profiles are of different devices: /device:TPU:2 before, /device:TPU:64 now
where the time goes in v1:
time: 60.3 us; the launch traced here: 60 us
  Pallas kernels  52.6 us (87%)
  local copies, waits for them, and re-layouts  6.74 us (11%)
  between operations  0.66 us (1%)
    pallas_call x1, Pallas kernels, body(): pl.pallas_call(functools.partial(kernel, dims, wscale), out_shape=(jax.Sh...  52.6 us
    unnamed x16, local copies, waits for them, and re-layouts  6.74 us

profile of v1, /device:TPU:64, one launch (start us, length us, event | category | flops | bytes accessed | tf_op | source)
XLA Modules:
  0.0 60.0 jit_solution(38520494043772168)
XLA Ops:
  0.6 0.0 copy-start.4
  0.6 0.7 %copy-done.4 = s32[1,64,3]{1,0,2:T(1,128)S(1)} copy-done((s32[1,64,3]{1,0,2:T(1,128)S(1)}, s32[1,64,3]{1,0,2:T(1,128)}, u32[]{:S(2)}) %copy-start.4) | copy-done | bytes 792
  1.3 0.6 copy.13
  1.9 52.6 %shard_map.101 = (bf16[256,1024]{1,0:T(8,128)(2,1)}, bf16[256,512]{1,0:T(8,128)(2,1)}, bf16[256,512]{1,0:T(8,128)(2,1)}, bf16[256,512]{1,0:T(8,128)(2,1)}, f32[16,1024]{1,0:T(8,128)}) custom-call(bf16[256,512]{1,0:T(8,128)(2,1)} %bitcast.18, bf16[256,512]{1,0:T(8,128)(2,1)} %bitcast.19, bf16[256,512]{1,0:T(8,128)(2,1)} %bitcast.20, ...), custom_call_target="tpu_custom_call" | custom-call | tf_op jit(solution)/shard_map/pallas_call | solution.py:304
  54.5 0.0 copy-start.2
  54.5 1.9 %copy.19 = bf16[1,256,1024]{2,1,0:T(8,128)(2,1)} copy(bf16[1,256,1024]{2,1,0:T(8,128)(2,1)} %bitcast.13) | data formatting | bytes 1048576
  56.4 0.0 copy-done.2
  56.4 0.0 copy-start.1
  56.4 0.7 %copy.20 = bf16[1,256,512]{2,1,0:T(8,128)(2,1)} copy(bf16[1,256,512]{2,1,0:T(8,128)(2,1)S(1)} %bitcast.17) | data formatting | bytes 524288
  57.1 0.3 copy-done.1
  57.4 0.0 copy-start
  57.4 0.7 %copy.21 = bf16[1,256,512]{2,1,0:T(8,128)(2,1)} copy(bf16[1,256,512]{2,1,0:T(8,128)(2,1)S(1)} %bitcast.16) | data formatting | bytes 524288
  58.1 0.3 copy-done
  58.5 0.0 copy-start.3
  58.5 0.7 %copy.22 = bf16[1,256,512]{2,1,0:T(8,128)(2,1)} copy(bf16[1,256,512]{2,1,0:T(8,128)(2,1)S(1)} %bitcast.15) | data formatting | bytes 524288
  59.2 0.2 copy-done.3
  59.3 0.6 %copy.23 = f32[16,1024]{1,0:T(8,128)} copy(f32[16,1024]{1,0:T(8,128)S(1)} %copy-done.3) | data formatting | bytes 131072
Async XLA Ops:
  0.6 0.7 %copy-start.4 = (s32[1,64,3]{1,0,2:T(1,128)S(1)}, s32[1,64,3]{1,0,2:T(1,128)}, u32[]{:S(2)}) copy-start(s32[1,64,3]{1,0,2:T(1,128)} %param.11) | copy-start | bytes 2308
  54.5 1.9 %copy-start.2 = (bf16[256,512]{1,0:T(8,128)(2,1)S(1)}, bf16[256,512]{1,0:T(8,128)(2,1)}, u32[]{:S(2)}) copy-start(bf16[256,512]{1,0:T(8,128)(2,1)} %get-tuple-element.11) | copy-start | bytes 786436
  56.4 1.0 %copy-start.1 = (bf16[256,512]{1,0:T(8,128)(2,1)S(1)}, bf16[256,512]{1,0:T(8,128)(2,1)}, u32[]{:S(2)}) copy-start(bf16[256,512]{1,0:T(8,128)(2,1)} %get-tuple-element.12) | copy-start | bytes 786436
  57.4 1.0 %copy-start = (bf16[256,512]{1,0:T(8,128)(2,1)S(1)}, bf16[256,512]{1,0:T(8,128)(2,1)}, u32[]{:S(2)}) copy-start(bf16[256,512]{1,0:T(8,128)(2,1)} %get-tuple-element.13) | copy-start | bytes 786436
  58.5 0.9 %copy-start.3 = (f32[16,1024]{1,0:T(8,128)S(1)}, f32[16,1024]{1,0:T(8,128)}, u32[]{:S(2)}) copy-start(f32[16,1024]{1,0:T(8,128)} %get-tuple-element.24) | copy-start | bytes 196612

commit v2 on v1

--- a/solution.py
+++ b/solution.py
@@ -38,12 +38,12 @@
 
 def kernel(
     dims, wscale,
-    q_hbm, k_hbm, v_hbm, g_hbm, w_hbm, mask,
-    out_s, dq_s, dk_s, dv_s, dw_out,
-    q_s, k_ext, v_ext, g_s, w_s, k_t, v_t, da_t, qbd, abd, p_t, at, dw_own,
-    csend, crecv, xsend, xrecv, ysend, yrecv, zsend, zrecv,
+    q_hbm, k_hbm, v_hbm, g_hbm, w_hbm, mask_hbm,
+    out_s, dq_s, dk_s, dv_s, dw_s,
+    mask, q_s, k_ext, v_ext, g_s, w_s, k_t, v_t, da_t, qbd, abd, p_t, at, dw_own,
+    csend, crecv, xsend, xrecv, zsend, zrecv, ysend, yrecv,
     dk_acc, dv_acc, gsend, grecv, dq_t,
-    lsem, h_s, h_r, c_s, c_r, x_s, x_r, y_s, y_r, z_s, z_r, a_s, a_r, g_ss, g_rs,
+    lsem, h_s, h_r, c_s, c_r, x_s, x_r, z_s, z_r, y_s, y_r, g_ss, g_rs,
 ):
     NY, ZH, ZL, NX = dims
     NZ = ZL * ZH
@@ -80,7 +80,8 @@
     load_q = pltpu.make_async_copy(q_hbm, q_s, lsem.at[2])
     load_k = pltpu.make_async_copy(k_hbm, k_ext.at[own], lsem.at[3])
     load_v = pltpu.make_async_copy(v_hbm, v_ext.at[own], lsem.at[4])
-    loads = [load_g, load_w, load_q, load_k, load_v]
+    load_m = pltpu.make_async_copy(mask_hbm, mask, lsem.at[5])
+    loads = [load_m, load_g, load_w, load_q, load_k, load_v]
     for copy in loads:
         copy.start()
 
@@ -88,18 +89,32 @@
 
     first, last = pl.ds(0, BLK), pl.ds(BLK, BLK)
     low, high = pl.ds(0, BLK), pl.ds(3 * BLK, BLK)
-    halo = [
-        remote(k_hbm.at[last], k_ext.at[low], h_s.at[0], h_r.at[0], right),
-        remote(k_hbm.at[first], k_ext.at[high], h_s.at[1], h_r.at[1], left),
-        remote(v_hbm.at[last], v_ext.at[low], h_s.at[2], h_r.at[2], right),
-        remote(v_hbm.at[first], v_ext.at[high], h_s.at[3], h_r.at[3], left),
-    ]
-    for copy in halo:
-        copy.start()
+
+    def halo_copies(g):
+        c = pl.ds(g * GW, GW)
+        return [
+            remote(k_hbm.at[last, c], k_ext.at[low, c], h_s.at[g, 0], h_r.at[g, 0], right),
+            remote(k_hbm.at[first, c], k_ext.at[high, c], h_s.at[g, 1], h_r.at[g, 1], left),
+            remote(v_hbm.at[last, c], v_ext.at[low, c], h_s.at[g, 2], h_r.at[g, 2], right),
+            remote(v_hbm.at[first, c], v_ext.at[high, c], h_s.at[g, 3], h_r.at[g, 3], left),
+        ]
+
+    for g in range(NG):
+        for copy in halo_copies(g):
+            copy.start()
 
     def cols(g):
         return slice(g * GW, (g + 1) * GW)
 
+    load_q.wait()
+    for b in range(2):
+        for g in range(NG):
+            scaled = q_s[b * BLK:(b + 1) * BLK, cols(g)] * jnp.asarray(HD ** -0.5, BF)
+            qbd[b, g] = block_diag(scaled)
+    load_v.wait()
+    v_t[:, BLK:3 * BLK] = v_ext[BLK:3 * BLK, :].T
+    load_k.wait()
+    k_t[:, BLK:3 * BLK] = k_ext[BLK:3 * BLK, :].T
     load_g.wait()
     load_w.wait()
     da = nt(g_s[...], w_s[...]).astype(BF)
@@ -107,32 +122,21 @@
         for g in range(NG):
             abd[b, g] = block_diag(da[b * BLK:(b + 1) * BLK, cols(g)])
     da_t[...] = nt(w_s[...], g_s[...]).astype(BF)
-    load_q.wait()
-    for b in range(2):
-        for g in range(NG):
-            scaled = q_s[b * BLK:(b + 1) * BLK, cols(g)] * jnp.asarray(HD ** -0.5, BF)
-            qbd[b, g] = block_diag(scaled)
-    load_k.wait()
-    load_v.wait()
-    k_t[:, BLK:3 * BLK] = k_ext[BLK:3 * BLK, :].T
-    v_t[:, BLK:3 * BLK] = v_ext[BLK:3 * BLK, :].T
-
+
+    load_m.wait()
     bias = []
     for b in range(2):
         row = ctx * 2 + b
-        bias.append([jnp.where(mask[c, row] == 1, 0.0, NEG).astype(F32) for c in (0, 2)])
-
-    for copy in halo:
-        copy.wait_recv()
-    k_t[:, :BLK] = k_ext[:BLK, :].T
-    k_t[:, 3 * BLK:] = k_ext[3 * BLK:, :].T
-    v_t[:, :BLK] = v_ext[:BLK, :].T
-    v_t[:, 3 * BLK:] = v_ext[3 * BLK:, :].T
+        bias.append([jnp.where(mask[c, 0, row] == 1, 0.0, NEG).astype(F32) for c in (0, 2)])
 
     def window(b):
         return slice(b * BLK, b * BLK + WIN)
 
     def forward(g):
+        for copy in halo_copies(g):
+            copy.wait_recv()
+        v_t[cols(g), :BLK] = v_ext[:BLK, cols(g)].T
+        v_t[cols(g), 3 * BLK:] = v_ext[3 * BLK:, cols(g)].T
         parts = []
         for b in range(2):
             s = nt(k_ext[window(b), cols(g)], qbd[b, g])
@@ -159,20 +163,16 @@
     def x_copy(g, d):
         return remote(xsend.at[g, (x + d) % NX], xrecv.at[g, d - 1], x_s.at[g, d - 1], x_r.at[g, d - 1], x_peer[d - 1])
 
-    def y_copy(g, d):
-        return remote(ysend.at[g, (y + d) % NY], yrecv.at[g, d - 1], y_s.at[g, d - 1], y_r.at[g, d - 1], y_peer[d - 1])
-
-    def z_copy(d):
-        return remote(zsend.at[(z + d) % ZL], zrecv.at[d - 1], z_s.at[d - 1], z_r.at[d - 1], z_peer[d - 1])
-
-    own_cols = pl.ds(pl.multiple_of(y * BLK, BLK), BLK)
-
-    def a_copy(d):
-        return remote(dw_out.at[:, own_cols], dw_out.at[:, own_cols], a_s.at[d - 1], a_r.at[d - 1], y_peer[d - 1])
-
-    def a_arrival(d):
-        there = pl.ds(pl.multiple_of(((y + NY - d) % NY) * BLK, BLK), BLK)
-        return remote(dw_out.at[:, own_cols], dw_out.at[:, there], a_s.at[d - 1], a_r.at[d - 1], y_peer[d - 1])
+    def z_copy(g, side):
+        t = side * ZL + g
+        slot = (t + NZ - z) % NZ - 1
+        return remote(zsend.at[g], zrecv.at[slot], z_s.at[g, side], z_r.at[slot], ident(y, t, x, core))
+
+    def z_arrival(slot):
+        return remote(zsend.at[0], zrecv.at[slot], z_s.at[0, 0], z_r.at[slot], z_peer[slot])
+
+    def y_copy(d):
+        return remote(ysend, yrecv.at[d - 1], y_s.at[d - 1], y_r.at[d - 1], y_peer[d - 1])
 
     def weight_part(g):
         mine = at[g, :, core].reshape(64, 2 * BLK)
@@ -189,36 +189,36 @@
         for d in range(1, NX):
             x_copy(g, d).start()
 
+    def z_each(g, act):
+        for side in range(ZH):
+            @pl.when(z != side * ZL + g)
+            def _():
+                act(z_copy(g, side))
+
     def x_sum(g):
         total = xsend[g, x].astype(F32)
         for d in range(1, NX):
             x_copy(g, d).wait_recv()
             total += xrecv[g, d - 1].astype(F32)
-        total = total.astype(BF)
-        for j in range(8):
-            ysend[g, j] = total[:, j * BLK:(j + 1) * BLK]
+        zsend[g] = total.astype(BF)
+        if g < ZL:
+            z_each(g, lambda copy: copy.start())
+
+    def z_sum():
+        total = zsend[z % ZL].astype(F32)
+        for slot in range(NZ - 1):
+            z_arrival(slot).wait_recv()
+            total += zrecv[slot].astype(F32)
+        ysend[...] = total.astype(BF)
         for d in range(1, NY):
-            y_copy(g, d).start()
-
-    def y_sum(g):
-        total = ysend[g, y].astype(F32)
+            y_copy(d).start()
+
+    def y_sum():
+        total = ysend[...].astype(F32)
         for d in range(1, NY):
-            y_copy(g, d).wait_recv()
-            total += yrecv[g, d - 1].astype(F32)
-        zsend[g] = total
-
-    def z_start():
-        for d in range(1, NZ):
-            z_copy(d).start()
-
-    def z_sum():
-        total = zsend[z % ZL]
-        for d in range(1, NZ):
-            z_copy(d).wait_recv()
-            total += zrecv[d - 1]
-        dw_out[:, own_cols] = total * wscale
-        for d in range(1, NY):
-            a_copy(d).start()
+            y_copy(d).wait_recv()
+            total += yrecv[d - 1].astype(F32)
+        dw_s[...] = total * wscale
 
     def grad_copy(side, g):
         return remote(gsend.at[side, g], grecv.at[side, g], g_ss.at[side, g], g_rs.at[side, g], right if side else left)
@@ -253,43 +253,54 @@
         weight_part(g)
         if g >= 1:
             core_sum(g - 1)
-    for g in range(NG):
-        backward(g)
-        if g == 0:
-            core_sum(NG - 1)
-        x_sum(g)
-        if g >= 1:
-            y_sum(g - 1)
-
+    k_t[:, :BLK] = k_ext[:BLK, :].T
+    k_t[:, 3 * BLK:] = k_ext[3 * BLK:, :].T
+    backward(0)
+    core_sum(NG - 1)
+    x_sum(0)
+    backward(1)
+    x_sum(1)
+    backward(2)
+    x_sum(2)
+    backward(3)
     dq_s[...] = dq_t[...].T
-    y_sum(NG - 1)
-    z_start()
+    x_sum(3)
     attn = at[...].reshape(NG * GW, 2 * BLK).T
     out_s[...] = nn(attn, w_s[...]).astype(BF)
-    z_sum()
     for g in range(NG):
         grad_copy(0, g).wait_recv()
         grad_copy(1, g).wait_recv()
         for n, (acc, dst) in enumerate(((dk_acc, dk_s), (dv_acc, dv_s))):
             dst[:BLK, cols(g)] = (acc[g, :BLK] + grecv[1, g, n].astype(F32)).astype(BF)
             dst[BLK:, cols(g)] = (acc[g, BLK:] + grecv[0, g, n].astype(F32)).astype(BF)
-    for d in range(1, NY):
-        a_arrival(d).wait_recv()
-
-    for copy in halo:
-        copy.wait_send()
+    z_sum()
+
     for g in range(NG):
+        for copy in halo_copies(g):
+            copy.wait_send()
         core_copy(g).wait_send()
         for d in range(1, NX):
             x_copy(g, d).wait_send()
-        for d in range(1, NY):
-            y_copy(g, d).wait_send()
+        if g < ZL:
+            z_each(g, lambda copy: copy.wait_send())
         grad_copy(0, g).wait_send()
         grad_copy(1, g).wait_send()
-    for d in range(1, NZ):
-        z_copy(d).wait_send()
+    y_sum()
     for d in range(1, NY):
-        a_copy(d).wait_send()
+        y_copy(d).wait_send()
+
+
+def store_kernel(*refs):
+    srcs, dsts, sem = refs[:5], refs[5:10], refs[10]
+    copies = [pltpu.make_async_copy(src, dst, sem.at[n]) for n, (src, dst) in enumerate(zip(srcs, dsts))]
+    for copy in copies:
+        copy.start()
+    for copy in copies:
+        copy.wait()
+
+
+def pinned(array, space):
+    return pltpu.with_memory_space_constraint(array, space)
 
 
 def body(dims, wscale, queries, keys, values, out_grad, w_out, block_mask):
@@ -297,22 +308,26 @@
     NZ = ZL * ZH
     tok, feat = queries.shape[1:]
     width = w_out.shape[1]
-    hbm = pl.BlockSpec(memory_space=pl.ANY)
+    free = pl.BlockSpec(memory_space=pl.ANY)
     vm = pltpu.VMEM
     dma = pltpu.SemaphoreType.DMA
     nx, ny, nz = max(NX - 1, 1), max(NY - 1, 1), max(NZ - 1, 1)
+    shapes = (
+        jax.ShapeDtypeStruct((tok, width), BF),
+        jax.ShapeDtypeStruct((tok, feat), BF),
+        jax.ShapeDtypeStruct((tok, feat), BF),
+        jax.ShapeDtypeStruct((tok, feat), BF),
+        jax.ShapeDtypeStruct((16, width), F32),
+    )
+    mask = jnp.transpose(block_mask, (2, 0, 1))
+    arrays = [pinned(a, pltpu.HBM) for a in (queries[0], keys[0], values[0], out_grad[0], w_out, mask)]
     outs = pl.pallas_call(
         functools.partial(kernel, dims, wscale),
-        out_shape=(
-            jax.ShapeDtypeStruct((tok, width), BF),
-            jax.ShapeDtypeStruct((tok, feat), BF),
-            jax.ShapeDtypeStruct((tok, feat), BF),
-            jax.ShapeDtypeStruct((tok, feat), BF),
-            jax.ShapeDtypeStruct((16, width), F32),
-        ),
-        in_specs=[hbm] * 5 + [pl.BlockSpec(memory_space=pltpu.SMEM)],
-        out_specs=[pl.BlockSpec(memory_space=pltpu.VMEM)] * 5,
+        out_shape=tuple(vm(a.shape, a.dtype) for a in shapes),
+        in_specs=[free] * 6,
+        out_specs=[pl.BlockSpec(memory_space=vm)] * 5,
         scratch_shapes=[
+            pltpu.SMEM((block_mask.shape[2], 1, block_mask.shape[1]), jnp.int32),
             vm((tok, feat), BF),
             vm((4 * BLK, feat), BF),
             vm((4 * BLK, feat), BF),
@@ -330,28 +345,34 @@
             vm((NG, 64, width), BF),
             vm((NG, 4, 16, width), BF),
             vm((NG, nx, 16, width), BF),
-            vm((NG, 8, 16, BLK), BF),
-            vm((NG, ny, 16, BLK), BF),
-            vm((NG, 16, BLK), F32),
-            vm((nz, 16, BLK), F32),
+            vm((NG, 16, width), BF),
+            vm((nz, 16, width), BF),
+            vm((16, width), BF),
+            vm((ny, 16, width), BF),
             vm((NG, tok, GW), F32),
             vm((NG, tok, GW), F32),
             vm((2, NG, 2, BLK, GW), BF),
             vm((2, NG, 2, BLK, GW), BF),
             vm((feat, tok), BF),
-            dma((5,)),
-            dma((4,)), dma((4,)),
+            dma((6,)),
+            dma((NG, 4)), dma((NG, 4)),
             dma((NG,)), dma((NG,)),
             dma((NG, nx)), dma((NG, nx)),
-            dma((NG, ny)), dma((NG, ny)),
-            dma((nz,)), dma((nz,)),
+            dma((NG, 2)), dma((nz,)),
             dma((ny,)), dma((ny,)),
             dma((2, NG)), dma((2, NG)),
         ],
         compiler_params=pltpu.CompilerParams(
-            collective_id=0, has_side_effects=True, vmem_limit_bytes=60 * 1024 * 1024
+            collective_id=0, has_side_effects=True, vmem_limit_bytes=40 * 1024 * 1024
         ),
-    )(queries[0], keys[0], values[0], out_grad[0], w_out, block_mask[0].T)
+    )(*arrays)
+    outs = pl.pallas_call(
+        store_kernel,
+        out_shape=shapes,
+        in_specs=[pl.BlockSpec(memory_space=vm)] * 5,
+        out_specs=[free] * 5,
+        scratch_shapes=[dma((5,))],
+    )(*[pinned(a, vm) for a in outs])
     return (outs[0][None], outs[1][None], outs[2][None], outs[3][None], outs[4])
 
 

time: 60.3 us -> 46.2 us (0.77)
  Pallas kernels: 52.6 us -> 45.4 us
  local copies, waits for them, and re-layouts: 6.74 us -> 0 us
    pallas_call x1 -> x2, Pallas kernels: 52.6 us -> 45.4 us  [the longest x1 44.3 us: body(): pl.pallas_call(functools.partial(kernel, dims, wscale), out_shape=tuple((...]
    unnamed x16 -> x0, local copies, waits for them, and re-layouts: 6.74 us -> none
where the time goes in v2:
time: 46.2 us; the launch traced here: 46.1 us
  Pallas kernels  45.4 us (98%)
  between operations  0.64 us (1%)
    pallas_call x1, Pallas kernels, body(): pl.pallas_call(functools.partial(kernel, dims, wscale), out_shape=tuple((...  44.3 us
    pallas_call x1, Pallas kernels, body(): pl.pallas_call(store_kernel, out_shape=shapes, in_specs=[pl.BlockSpec(mem...  1.11 us

profile of v2, /device:TPU:64, one launch (start us, length us, event | category | flops | bytes accessed | tf_op | source)
XLA Modules:
  0.0 46.1 jit_solution(2512997331585603701)
XLA Ops:
  0.6 44.3 %shard_map.101 = (bf16[256,1024]{1,0:T(8,128)(2,1)S(1)}, bf16[256,512]{1,0:T(8,128)(2,1)S(1)}, bf16[256,512]{1,0:T(8,128)(2,1)S(1)}, bf16[256,512]{1,0:T(8,128)(2,1)S(1)}, f32[16,1024]{1,0:T(8,128)S(1)}) custom-call(bf16[256,512]{1,0:T(8,128)(2,1)} %bitcast.10, bf16[256,512]{1,0:T(8,128)(2,1)} %bitcast.11, bf16[256,512]{1,0:T(8,128)(2,1)} %bitcast.12, ...), custom_call_target="tpu_custom_call" | custom-call | tf_op jit(solution)/shard_map/pallas_call | solution.py:324
  45.0 1.1 %shard_map.102 = (bf16[256,1024]{1,0:T(8,128)(2,1)}, bf16[256,512]{1,0:T(8,128)(2,1)}, bf16[256,512]{1,0:T(8,128)(2,1)}, bf16[256,512]{1,0:T(8,128)(2,1)}, f32[16,1024]{1,0:T(8,128)}) custom-call(bf16[256,1024]{1,0:T(8,128)(2,1)S(1)} %get-tuple-element.15.refs_0_, bf16[256,512]{1,0:T(8,128)(2,1)S(1)} %get-tuple-element.16.refs_1_, ...), custom_call_target="tpu_custom_call" | custom-call | tf_op jit(solution)/shard_map/pallas_call | solution.py:369

commit v3 on v2

--- a/solution.py
+++ b/solution.py
@@ -40,7 +40,7 @@
     dims, wscale,
     q_hbm, k_hbm, v_hbm, g_hbm, w_hbm, mask_hbm,
     out_s, dq_s, dk_s, dv_s, dw_s,
-    mask, q_s, k_ext, v_ext, g_s, w_s, k_t, v_t, da_t, qbd, abd, p_t, at, dw_own,
+    mask, q_s, k_ext, v_ext, g_s, w_s, k_t, v_t, da_t, qbd, abd, e_own, e_halo, o_own, stats, at, dw_own,
     csend, crecv, xsend, xrecv, zsend, zrecv, ysend, yrecv,
     dk_acc, dv_acc, gsend, grecv, dq_t,
     lsem, h_s, h_r, c_s, c_r, x_s, x_r, z_s, z_r, y_s, y_r, g_ss, g_rs,
@@ -69,11 +69,6 @@
             src_ref=src, dst_ref=dst, send_sem=ssem, recv_sem=rsem, device_id=dev, device_id_type=MESH
         )
 
-    barrier = pltpu.get_barrier_semaphore()
-    peers = [right, left] + x_peer + y_peer + z_peer
-    for dev in peers:
-        pl.semaphore_signal(barrier, inc=1, device_id=dev, device_id_type=MESH)
-
     own = pl.ds(BLK, 2 * BLK)
     load_g = pltpu.make_async_copy(g_hbm, g_s, lsem.at[0])
     load_w = pltpu.make_async_copy(w_hbm, w_s, lsem.at[1])
@@ -81,79 +76,101 @@
     load_k = pltpu.make_async_copy(k_hbm, k_ext.at[own], lsem.at[3])
     load_v = pltpu.make_async_copy(v_hbm, v_ext.at[own], lsem.at[4])
     load_m = pltpu.make_async_copy(mask_hbm, mask, lsem.at[5])
-    loads = [load_m, load_g, load_w, load_q, load_k, load_v]
+    loads = [load_q, load_m, load_v, load_k, load_g, load_w]
     for copy in loads:
         copy.start()
 
+    barrier = pltpu.get_barrier_semaphore()
+    peers = [right, left] + x_peer + y_peer + z_peer
+    for dev in peers:
+        pl.semaphore_signal(barrier, inc=1, device_id=dev, device_id_type=MESH)
+
     pl.semaphore_wait(barrier, len(peers))
 
     first, last = pl.ds(0, BLK), pl.ds(BLK, BLK)
     low, high = pl.ds(0, BLK), pl.ds(3 * BLK, BLK)
 
-    def halo_copies(g):
+    def halo_copy(n, g):
         c = pl.ds(g * GW, GW)
-        return [
-            remote(k_hbm.at[last, c], k_ext.at[low, c], h_s.at[g, 0], h_r.at[g, 0], right),
-            remote(k_hbm.at[first, c], k_ext.at[high, c], h_s.at[g, 1], h_r.at[g, 1], left),
-            remote(v_hbm.at[last, c], v_ext.at[low, c], h_s.at[g, 2], h_r.at[g, 2], right),
-            remote(v_hbm.at[first, c], v_ext.at[high, c], h_s.at[g, 3], h_r.at[g, 3], left),
-        ]
-
-    for g in range(NG):
-        for copy in halo_copies(g):
-            copy.start()
+        src, dst = (k_hbm, k_ext) if n < 2 else (v_hbm, v_ext)
+        if n % 2:
+            return remote(src.at[first, c], dst.at[high, c], h_s.at[g, n], h_r.at[g, n], left)
+        return remote(src.at[last, c], dst.at[low, c], h_s.at[g, n], h_r.at[g, n], right)
+
+    def halo_send(g):
+        for n in range(4):
+            halo_copy(n, g).start()
+
+    halo_send(0)
 
     def cols(g):
         return slice(g * GW, (g + 1) * GW)
+
+    def rows_of(stat):
+        return jnp.concatenate(
+            [jnp.broadcast_to(stat[:, :BLK], (HD, BLK)), jnp.broadcast_to(stat[:, BLK:], (HD, BLK))], axis=0
+        )
 
     load_q.wait()
     for b in range(2):
         for g in range(NG):
             scaled = q_s[b * BLK:(b + 1) * BLK, cols(g)] * jnp.asarray(HD ** -0.5, BF)
             qbd[b, g] = block_diag(scaled)
-    load_v.wait()
-    v_t[:, BLK:3 * BLK] = v_ext[BLK:3 * BLK, :].T
-    load_k.wait()
-    k_t[:, BLK:3 * BLK] = k_ext[BLK:3 * BLK, :].T
-    load_g.wait()
-    load_w.wait()
-    da = nt(g_s[...], w_s[...]).astype(BF)
-    for b in range(2):
-        for g in range(NG):
-            abd[b, g] = block_diag(da[b * BLK:(b + 1) * BLK, cols(g)])
-    da_t[...] = nt(w_s[...], g_s[...]).astype(BF)
-
     load_m.wait()
     bias = []
     for b in range(2):
         row = ctx * 2 + b
         bias.append([jnp.where(mask[c, 0, row] == 1, 0.0, NEG).astype(F32) for c in (0, 2)])
+    load_v.wait()
+    v_t[:, BLK:3 * BLK] = v_ext[BLK:3 * BLK, :].T
+    load_k.wait()
+
+    def own_part(g):
+        for b in range(2):
+            s = nt(k_ext[BLK:3 * BLK, cols(g)], qbd[b, g])
+            mid, other = s[b * BLK:(b + 1) * BLK], s[(1 - b) * BLK:(2 - b) * BLK]
+            b_other = bias[b][1 - b]
+            top = jnp.maximum(jnp.max(mid, axis=0, keepdims=True), jnp.max(other, axis=0, keepdims=True) + b_other)
+            e_mid = jnp.exp(mid - top)
+            e_other = jnp.exp(other - (top - b_other))
+            total = jnp.sum(e_mid + e_other, axis=0, keepdims=True)
+            pair = (e_mid, e_other) if b == 0 else (e_other, e_mid)
+            e = jnp.concatenate(pair, axis=0).astype(BF)
+            e_own[b, g] = e
+            o_own[b, g] = diagonal(nn(v_t[cols(g), BLK:3 * BLK], e))
+            stats[b, g, 0:1] = top
+            stats[b, g, 1:2] = total
 
     def window(b):
         return slice(b * BLK, b * BLK + WIN)
 
+    def halo_at(b):
+        return slice(3 * b * BLK, 3 * b * BLK + BLK)
+
     def forward(g):
-        for copy in halo_copies(g):
-            copy.wait_recv()
-        v_t[cols(g), :BLK] = v_ext[:BLK, cols(g)].T
-        v_t[cols(g), 3 * BLK:] = v_ext[3 * BLK:, cols(g)].T
         parts = []
+        for n in range(2):
+            halo_copy(n, g).wait_recv()
+        exps = []
         for b in range(2):
-            s = nt(k_ext[window(b), cols(g)], qbd[b, g])
-            lo, mid, hi = s[:BLK], s[BLK:2 * BLK], s[2 * BLK:]
-            b_lo, b_hi = bias[b]
-            top = jnp.maximum(
-                jnp.max(mid, axis=0, keepdims=True),
-                jnp.maximum(jnp.max(lo, axis=0, keepdims=True) + b_lo, jnp.max(hi, axis=0, keepdims=True) + b_hi),
-            )
-            e_lo = jnp.exp(lo - (top - b_lo))
-            e_mid = jnp.exp(mid - top)
-            e_hi = jnp.exp(hi - (top - b_hi))
-            total = jnp.sum(e_lo + e_mid + e_hi, axis=0, keepdims=True)
-            inv = 1.0 / total
-            p = jnp.concatenate([(e_lo * inv).astype(BF), (e_mid * inv).astype(BF), (e_hi * inv).astype(BF)], axis=0)
-            p_t[b, g] = p
-            parts.append(diagonal(nn(v_t[cols(g), window(b)], p)).astype(BF))
+            s = nt(k_ext[halo_at(b), cols(g)], qbd[b, g])
+            b_halo = bias[b][b]
+            top_own = stats[b, g, 0:1]
+            top = jnp.maximum(top_own, jnp.max(s, axis=0, keepdims=True) + b_halo)
+            e = jnp.exp(s - (top - b_halo))
+            shrink = jnp.exp(top_own - top)
+            inv = 1.0 / (stats[b, g, 1:2] * shrink + jnp.sum(e, axis=0, keepdims=True))
+            e = e.astype(BF)
+            e_halo[b, g] = e
+            stats[b, g, 2:3] = shrink * inv
+            stats[b, g, 3:4] = inv
+            exps.append((e, shrink * inv, inv))
+        for n in range(2, 4):
+            halo_copy(n, g).wait_recv()
+        for b in range(2):
+            e, f_own, f_halo = exps[b]
+            o_halo = diagonal(nn(v_ext[halo_at(b), cols(g)].T, e))
+            parts.append((o_own[b, g] * rows_of(f_own) + o_halo * rows_of(f_halo)).astype(BF))
         rows = jnp.concatenate(parts, axis=1)
         at[g] = rows.reshape(4, 2, 16, 2 * BLK)
 
@@ -171,8 +188,24 @@
     def z_arrival(slot):
         return remote(zsend.at[0], zrecv.at[slot], z_s.at[0, 0], z_r.at[slot], z_peer[slot])
 
-    def y_copy(d):
+    def z_each(g, act):
+        for side in range(ZH):
+            @pl.when(z != side * ZL + g)
+            def _():
+                act(z_copy(g, side))
+
+    def y_copy(j):
+        slot = (j + NY - y) % NY - 1
+        return remote(ysend, yrecv.at[slot], y_s.at[slot], y_r.at[slot], ident(j, z, x, core))
+
+    def y_arrival(d):
         return remote(ysend, yrecv.at[d - 1], y_s.at[d - 1], y_r.at[d - 1], y_peer[d - 1])
+
+    def y_each(act):
+        for j in range(NY):
+            @pl.when(y != j)
+            def _():
+                act(y_copy(j))
 
     def weight_part(g):
         mine = at[g, :, core].reshape(64, 2 * BLK)
@@ -186,14 +219,8 @@
         core_copy(g).wait_recv()
         total = dw_own[g] + crecv[g].astype(F32)
         xsend[g] = total.astype(BF).reshape(4, 16, 1024)
-        for d in range(1, NX):
+        for d in sorted(range(1, NX), key=lambda d: -min(d, NX - d)):
             x_copy(g, d).start()
-
-    def z_each(g, act):
-        for side in range(ZH):
-            @pl.when(z != side * ZL + g)
-            def _():
-                act(z_copy(g, side))
 
     def x_sum(g):
         total = xsend[g, x].astype(F32)
@@ -201,22 +228,22 @@
             x_copy(g, d).wait_recv()
             total += xrecv[g, d - 1].astype(F32)
         zsend[g] = total.astype(BF)
-        if g < ZL:
-            z_each(g, lambda copy: copy.start())
-
-    def z_sum():
-        total = zsend[z % ZL].astype(F32)
-        for slot in range(NZ - 1):
-            z_arrival(slot).wait_recv()
-            total += zrecv[slot].astype(F32)
-        ysend[...] = total.astype(BF)
-        for d in range(1, NY):
-            y_copy(d).start()
+        z_each(g, lambda copy: copy.start())
+
+    def z_sum(g):
+        @pl.when(z % ZL == g)
+        def _():
+            total = zsend[g].astype(F32)
+            for slot in range(NZ - 1):
+                z_arrival(slot).wait_recv()
+                total += zrecv[slot].astype(F32)
+            ysend[...] = total.astype(BF)
+            y_each(lambda copy: copy.start())
 
     def y_sum():
         total = ysend[...].astype(F32)
         for d in range(1, NY):
-            y_copy(d).wait_recv()
+            y_arrival(d).wait_recv()
             total += yrecv[d - 1].astype(F32)
         dw_s[...] = total * wscale
 
@@ -234,8 +261,11 @@
                 [jnp.sum(prod[:HD], axis=0, keepdims=True), jnp.sum(prod[HD:], axis=0, keepdims=True)], axis=1
             )
             dp_t = nt(v_ext[window(b), cols(g)], abd[b, g])
-            p = p_t[b, g]
-            ds = (p.astype(F32) * (dp_t - delta)).astype(BF)
+            p_own = e_own[b, g].astype(F32) * stats[b, g, 2:3]
+            p_halo = e_halo[b, g].astype(F32) * stats[b, g, 3:4]
+            p_all = jnp.concatenate((p_halo, p_own) if b == 0 else (p_own, p_halo), axis=0)
+            p = p_all.astype(BF)
+            ds = (p_all * (dp_t - delta)).astype(BF)
             v_win.append(nn(p, abd[b, g]))
             k_win.append(nn(ds, qbd[b, g]))
             q_parts.append((diagonal(nn(k_t[cols(g), window(b)], ds)) * (HD ** -0.5)).astype(BF))
@@ -248,46 +278,66 @@
         dv_acc[g] = v_win[0][BLK:] + v_win[1][:2 * BLK]
         dq_t[cols(g), :] = jnp.concatenate(q_parts, axis=1)
 
-    for g in range(NG):
-        forward(g)
-        weight_part(g)
-        if g >= 1:
-            core_sum(g - 1)
-    k_t[:, :BLK] = k_ext[:BLK, :].T
-    k_t[:, 3 * BLK:] = k_ext[3 * BLK:, :].T
+    own_part(0)
+    halo_send(1)
+    own_part(1)
+    halo_send(2)
+    halo_send(3)
+    own_part(2)
+    load_g.wait()
+    forward(0)
+    weight_part(0)
+    own_part(3)
+    forward(1)
+    weight_part(1)
+    core_sum(0)
+    forward(2)
+    weight_part(2)
+    core_sum(1)
+    forward(3)
+    weight_part(3)
+    core_sum(2)
+    load_w.wait()
+    da = nt(g_s[...], w_s[...]).astype(BF)
+    for b in range(2):
+        for g in range(NG):
+            abd[b, g] = block_diag(da[b * BLK:(b + 1) * BLK, cols(g)])
+    core_sum(3)
+    da_t[...] = nt(w_s[...], g_s[...]).astype(BF)
+    k_t[...] = k_ext[...].T
+    x_sum(0)
     backward(0)
-    core_sum(NG - 1)
-    x_sum(0)
+    x_sum(1)
     backward(1)
-    x_sum(1)
+    x_sum(2)
+    x_sum(3)
     backward(2)
-    x_sum(2)
+    z_sum(0)
     backward(3)
-    dq_s[...] = dq_t[...].T
-    x_sum(3)
+    z_sum(1)
     attn = at[...].reshape(NG * GW, 2 * BLK).T
     out_s[...] = nn(attn, w_s[...]).astype(BF)
+    z_sum(2)
+    dq_s[...] = dq_t[...].T
+    z_sum(3)
+
     for g in range(NG):
         grad_copy(0, g).wait_recv()
         grad_copy(1, g).wait_recv()
         for n, (acc, dst) in enumerate(((dk_acc, dk_s), (dv_acc, dv_s))):
             dst[:BLK, cols(g)] = (acc[g, :BLK] + grecv[1, g, n].astype(F32)).astype(BF)
             dst[BLK:, cols(g)] = (acc[g, BLK:] + grecv[0, g, n].astype(F32)).astype(BF)
-    z_sum()
-
     for g in range(NG):
-        for copy in halo_copies(g):
-            copy.wait_send()
+        for n in range(4):
+            halo_copy(n, g).wait_send()
         core_copy(g).wait_send()
         for d in range(1, NX):
             x_copy(g, d).wait_send()
-        if g < ZL:
-            z_each(g, lambda copy: copy.wait_send())
+        z_each(g, lambda copy: copy.wait_send())
         grad_copy(0, g).wait_send()
         grad_copy(1, g).wait_send()
     y_sum()
-    for d in range(1, NY):
-        y_copy(d).wait_send()
+    y_each(lambda copy: copy.wait_send())
 
 
 def store_kernel(*refs):
@@ -338,7 +388,10 @@
             vm((feat, tok), BF),
             vm((2, NG, 2 * BLK, GW), BF),
             vm((2, NG, 2 * BLK, GW), BF),
-            vm((2, NG, WIN, 2 * BLK), BF),
+            vm((2, NG, 2 * BLK, 2 * BLK), BF),
+            vm((2, NG, BLK, 2 * BLK), BF),
+            vm((2, NG, GW, BLK), F32),
+            vm((2, NG, 8, 2 * BLK), F32),
             vm((NG, 4, 2, 16, tok), BF),
             vm((NG, 64, width), F32),
             vm((NG, 64, width), BF),

time: 46.2 us -> 41.5 us (0.90)
  the two profiles are of different devices: /device:TPU:64 before, /device:TPU:192 now
where the time goes in v3:
time: 41.5 us; the launch traced here: 41.4 us
  Pallas kernels  40.8 us (98%)
  between operations  0.64 us (2%)
    pallas_call x1, Pallas kernels, body(): pl.pallas_call(functools.partial(kernel, dims, wscale), out_shape=tuple((...  39.7 us
    pallas_call x1, Pallas kernels, body(): pl.pallas_call(store_kernel, out_shape=shapes, in_specs=[pl.BlockSpec(mem...  1.11 us

profile of v3, /device:TPU:192, one launch (start us, length us, event | category | flops | bytes accessed | tf_op | source)
XLA Modules:
  0.0 41.4 jit_solution(10558668256485196599)
XLA Ops:
  0.6 39.7 %shard_map.101 = (bf16[256,1024]{1,0:T(8,128)(2,1)S(1)}, bf16[256,512]{1,0:T(8,128)(2,1)S(1)}, bf16[256,512]{1,0:T(8,128)(2,1)S(1)}, bf16[256,512]{1,0:T(8,128)(2,1)S(1)}, f32[16,1024]{1,0:T(8,128)S(1)}) custom-call(bf16[256,512]{1,0:T(8,128)(2,1)} %bitcast.10, bf16[256,512]{1,0:T(8,128)(2,1)} %bitcast.11, bf16[256,512]{1,0:T(8,128)(2,1)} %bitcast.12, ...), custom_call_target="tpu_custom_call" | custom-call | tf_op jit(solution)/shard_map/pallas_call | solution.py:374
  40.3 1.1 %shard_map.102 = (bf16[256,1024]{1,0:T(8,128)(2,1)}, bf16[256,512]{1,0:T(8,128)(2,1)}, bf16[256,512]{1,0:T(8,128)(2,1)}, bf16[256,512]{1,0:T(8,128)(2,1)}, f32[16,1024]{1,0:T(8,128)}) custom-call(bf16[256,1024]{1,0:T(8,128)(2,1)S(1)} %get-tuple-element.15.refs_0_, bf16[256,512]{1,0:T(8,128)(2,1)S(1)} %get-tuple-element.16.refs_1_, ...), custom_call_target="tpu_custom_call" | custom-call | tf_op jit(solution)/shard_map/pallas_call | solution.py:422

commit v4 on v3

--- a/solution.py
+++ b/solution.py
@@ -272,8 +272,6 @@
         for n, win in enumerate((k_win, v_win)):
             gsend[0, g, n] = win[0][:BLK].astype(BF)
             gsend[1, g, n] = win[1][2 * BLK:].astype(BF)
-        grad_copy(0, g).start()
-        grad_copy(1, g).start()
         dk_acc[g] = k_win[0][BLK:] + k_win[1][:2 * BLK]
         dv_acc[g] = v_win[0][BLK:] + v_win[1][:2 * BLK]
         dq_t[cols(g), :] = jnp.concatenate(q_parts, axis=1)
@@ -314,6 +312,9 @@
     backward(2)
     z_sum(0)
     backward(3)
+    for g in range(NG):
+        grad_copy(0, g).start()
+        grad_copy(1, g).start()
     z_sum(1)
     attn = at[...].reshape(NG * GW, 2 * BLK).T
     out_s[...] = nn(attn, w_s[...]).astype(BF)

time: 41.5 us -> 41.3 us (level)
  the two profiles are of different devices: /device:TPU:192 before, /device:TPU:1 now
where the time goes in v4:
time: 41.3 us; the launch traced here: 41.2 us
  Pallas kernels  40.5 us (98%)
  between operations  0.64 us (2%)
    pallas_call x1, Pallas kernels, body(): pl.pallas_call(functools.partial(kernel, dims, wscale), out_shape=tuple((...  39.4 us
    pallas_call x1, Pallas kernels, body(): pl.pallas_call(store_kernel, out_shape=shapes, in_specs=[pl.BlockSpec(mem...  1.11 us

profile of v4, /device:TPU:1, one launch (start us, length us, event | category | flops | bytes accessed | tf_op | source)
XLA Modules:
  0.0 41.2 jit_solution(945461402785716220)
XLA Ops:
  0.6 39.4 %shard_map.101 = (bf16[256,1024]{1,0:T(8,128)(2,1)S(1)}, bf16[256,512]{1,0:T(8,128)(2,1)S(1)}, bf16[256,512]{1,0:T(8,128)(2,1)S(1)}, bf16[256,512]{1,0:T(8,128)(2,1)S(1)}, f32[16,1024]{1,0:T(8,128)S(1)}) custom-call(bf16[256,512]{1,0:T(8,128)(2,1)} %bitcast.10, bf16[256,512]{1,0:T(8,128)(2,1)} %bitcast.11, bf16[256,512]{1,0:T(8,128)(2,1)} %bitcast.12, ...), custom_call_target="tpu_custom_call" | custom-call | tf_op jit(solution)/shard_map/pallas_call | solution.py:375
  40.1 1.1 %shard_map.102 = (bf16[256,1024]{1,0:T(8,128)(2,1)}, bf16[256,512]{1,0:T(8,128)(2,1)}, bf16[256,512]{1,0:T(8,128)(2,1)}, bf16[256,512]{1,0:T(8,128)(2,1)}, f32[16,1024]{1,0:T(8,128)}) custom-call(bf16[256,1024]{1,0:T(8,128)(2,1)S(1)} %get-tuple-element.15.refs_0_, bf16[256,512]{1,0:T(8,128)(2,1)S(1)} %get-tuple-element.16.refs_1_, ...), custom_call_target="tpu_custom_call" | custom-call | tf_op jit(solution)/shard_map/pallas_call | solution.py:423
